TPU v7x, 32 devices: a whole 2x2x4 slice. The times are simulated.
32 devices in a mesh: groups: 2 (over x), gx: 4 (over y, core), gy: 4 (over z).
Axes of the slice: x: 2, y: 2, z: 4, core: 2. Of those that a mesh axis runs over, the one named last changes fastest.
Arguments:
- inputs: bfloat16 [32, 16, 58, 128], P(('groups', 'gx'), 'gy'), parts along dimension 0, may hold values from -6 to 6
- target: bfloat16 [32, 16, 53, 128], P(('groups', 'gx'), 'gy'), parts along dimension 0, may hold values from -6 to 6
- w_first: bfloat16 [3, 3, 3, 58, 64], replicated, may hold values from -0.15625 to 0.15625
- w_second: bfloat16 [3, 3, 3, 64, 53], replicated, may hold values from -0.15625 to 0.15625
Outputs:
- prediction: bfloat16 [32, 16, 53, 128], P(('groups', 'gx'), 'gy'), parts along dimension 0
- grad_first: float32 [6, 3, 3, 58, 64], P('groups'), parts along dimension 0
- grad_second: float32 [6, 3, 3, 64, 53], P('groups'), parts along dimension 0
There are 2 independent parts, one for each index of `groups`. A program takes and returns all parts, laid end to end along the dimension named above; an argument that names none is the same for every part. Nothing has to cross between parts.
All inputs are finite; a program needn't handle non-finite values.
Results may differ from a plain program's by a relative error of at most 0.0049.
Values may be sent and summed in bfloat16 or wider, within the bound.
A program may use at most 64 MiB of HBM per device.

v0:
```python
import math
import jax
import jax.numpy as jnp
from jax import lax
from jax.sharding import PartitionSpec as P

root_two_pi = 0.7978845608028654
cubic_term = 0.044715


def extended(cells, sides, width):
    for axis, dim in sides:
        count = lax.axis_size(axis)
        ends = count - 1
        head = lax.slice_in_dim(cells, 0, width, axis=dim)
        tail = lax.slice_in_dim(cells, cells.shape[dim] - width, cells.shape[dim], axis=dim)
        cells = jnp.concatenate(
            [
                lax.ppermute(tail, axis, [(i, (i + 1) % count) for i in range(ends)]),
                cells,
                lax.ppermute(head, axis, [((i + 1) % count, i) for i in range(ends)]),
            ],
            axis=dim,
        )
    return cells


def shifted(value, axis, steps):
    count = lax.axis_size(axis)
    leading, last = (max(0, -steps), min(count, count - steps))
    return lax.ppermute(value, axis, [(source, source + steps) for source in range(leading, last)])


def smooth_gate(activation):
    tangent = jnp.tanh(
        root_two_pi * (activation + cubic_term * activation * activation * activation)
    )
    return 0.5 * activation * (1.0 + tangent)


def gate_slope(activation):
    tangent = jnp.tanh(
        root_two_pi * (activation + cubic_term * activation * activation * activation)
    )
    return 0.5 * (1.0 + tangent) + 0.5 * activation * (1.0 - tangent * tangent) * root_two_pi * (
        1.0 + 3.0 * cubic_term * activation * activation
    )


def depth_padded(field):
    return jnp.pad(field, ((0, 0), (0, 0), (0, 0), (1, 1)))


def correlate(field, kernel):
    extent_x = field.shape[0] - 2
    extent_y = field.shape[1] - 2
    depth = field.shape[3]
    padded = depth_padded(field)
    total = jnp.zeros((extent_x, extent_y, kernel.shape[4], depth), jnp.float32)
    for step_a in range(3):
        for step_b in range(3):
            for step_c in range(3):
                window = padded[
                    step_a : step_a + extent_x,
                    step_b : step_b + extent_y,
                    :,
                    step_c : step_c + depth,
                ]
                total = total + jnp.einsum(
                    "xycz,co->xyoz",
                    window,
                    kernel[step_a, step_b, step_c],
                    preferred_element_type=jnp.float32,
                )
    return total


def correlate_back(field, kernel):
    extent_x = field.shape[0] - 2
    extent_y = field.shape[1] - 2
    depth = field.shape[3]
    padded = depth_padded(field)
    total = jnp.zeros((extent_x, extent_y, kernel.shape[3], depth), jnp.float32)
    for step_a in range(3):
        for step_b in range(3):
            for step_c in range(3):
                window = padded[
                    2 - step_a : 2 - step_a + extent_x,
                    2 - step_b : 2 - step_b + extent_y,
                    :,
                    2 - step_c : 2 - step_c + depth,
                ]
                total = total + jnp.einsum(
                    "xyoz,io->xyiz",
                    window,
                    kernel[step_a, step_b, step_c],
                    preferred_element_type=jnp.float32,
                )
    return total


def filter_grad(field, slope_term):
    extent_x = slope_term.shape[0]
    extent_y = slope_term.shape[1]
    depth = slope_term.shape[3]
    padded = depth_padded(field)
    planes = []
    for step_a in range(3):
        rows_b = []
        for step_b in range(3):
            rows_c = []
            for step_c in range(3):
                window = padded[
                    step_a : step_a + extent_x,
                    step_b : step_b + extent_y,
                    :,
                    step_c : step_c + depth,
                ]
                rows_c.append(
                    jnp.einsum(
                        "xycz,xyoz->co", window, slope_term, preferred_element_type=jnp.float32
                    )
                )
            rows_b.append(jnp.stack(rows_c))
        planes.append(jnp.stack(rows_b))
    return jnp.stack(planes)


def on_device(inputs, target, w_first, w_second):
    block_x = inputs.shape[0]
    block_y = inputs.shape[1]
    padded_in = extended(inputs, (("gx", 0), ("gy", 1)), 1)
    activation = correlate(padded_in, w_first)
    hidden = smooth_gate(activation).astype(jnp.bfloat16)
    padded_hidden = extended(hidden, (("gx", 0), ("gy", 1)), 1)
    output = correlate(padded_hidden, w_second)
    prediction = output.astype(jnp.bfloat16)
    cell_count = block_x * lax.axis_size("gx") * block_y * lax.axis_size("gy") * inputs.shape[3]
    normalizer = 1.0 / math.sqrt(cell_count)
    output_grad = ((output - target.astype(jnp.float32)) * normalizer).astype(jnp.bfloat16)
    grad_second = filter_grad(padded_hidden, output_grad)
    widened = jnp.pad(output_grad, ((2, 2), (2, 2), (0, 0), (0, 0)))
    spread = correlate_back(widened, w_second)
    extent_x = spread.shape[0]
    from_below = shifted(spread[extent_x - 1 :].astype(jnp.bfloat16), "gx", 1).astype(jnp.float32)
    from_above = shifted(spread[:1].astype(jnp.bfloat16), "gx", -1).astype(jnp.float32)
    summed_x = spread[1 : extent_x - 1]
    summed_x = summed_x.at[:1].add(from_below).at[-1:].add(from_above)
    extent_y = summed_x.shape[1]
    from_left = shifted(summed_x[:, extent_y - 1 :].astype(jnp.bfloat16), "gy", 1).astype(
        jnp.float32
    )
    from_right = shifted(summed_x[:, :1].astype(jnp.bfloat16), "gy", -1).astype(jnp.float32)
    back_grad = summed_x[:, 1 : extent_y - 1].at[:, :1].add(from_left).at[:, -1:].add(from_right)
    slope_term = (back_grad * gate_slope(activation)).astype(jnp.bfloat16)
    grad_first = filter_grad(padded_in, slope_term)
    grad_first, grad_second = lax.psum((grad_first, grad_second), ("gx", "gy"))
    return (prediction, grad_first, grad_second)


def solution(mesh):
    placed = (
        P(("groups", "gx"), "gy", None, None),
        P(("groups", "gx"), "gy", None, None),
        P(),
        P(),
    )
    return jax.shard_map(
        on_device,
        mesh=mesh,
        in_specs=placed,
        out_specs=(
            P(("groups", "gx"), "gy", None, None),
            P("groups", None, None, None, None),
            P("groups", None, None, None, None),
        ),
        check_vma=False,
    )
```

profile of v0, /device:TPU:0, one launch (start us, length us, event | category | flops | bytes accessed | tf_op | source)
XLA Modules:
  0.0 207.4 jit_solution(16586595825704326842)
XLA Ops:
  7.2 0.9 fusion.357
  8.2 2.4 %collective-permute-start = (bf16[1,4,58,128]{3,2,1,0:T(8,128)(2,1)S(1)}, bf16[1,4,58,128]{3,2,1,0:T(8,128)(2,1)S(1)}, u32[]{:S(2)}, u32[]{:S(2)}) collective-permute-start(bf16[1,4,58,128]{3,2,1,0:T(8,128)(2,1)S(1)} %copy.188), channel_id=1, source_target_pairs={{0,4},{4,8},{8,12},{1,5},{5,9},{9,13},{2,6},{6,10},{10,14},{3,7},{... | collective-permute-start | bytes 178184 | tf_op jit(solution)/shard_map/ppermute | solution.py:19
  10.6 1.3 collective-permute-start.1
  11.9 1.2 constant_dynamic-update-slice_fusion.6
  13.1 2.8 %collective-permute-done.1 = bf16[1,4,58,128]{3,2,1,0:T(8,128)(2,1)S(1)} collective-permute-done((bf16[1,4,58,128]{3,2,1,0:T(8,128)(2,1)S(1)}, bf16[1,4,58,128]{3,2,1,0:T(8,128)(2,1)S(1)}, u32[]{:S(2)}, u32[]{:S(2)}) %collective-permute-start.1) | collective-permute-done | bytes 59424 | tf_op jit(solution)/shard_map/ppermute | solution.py:21
  15.9 3.5 %collective-permute-start.2 = (bf16[6,1,58,128]{3,2,1,0:T(8,128)(2,1)S(1)}, bf16[6,1,58,128]{3,2,1,0:T(8,128)(2,1)S(1)}, u32[]{:S(2)}, u32[]{:S(2)}) collective-permute-start(bf16[6,1,58,128]{3,2,1,0:T(8,128)(2,1)S(1)} %get-tuple-element.64), channel_id=1, source_target_pairs={{0,1},{1,2},{2,3},{4,5},{5,6},{6,7},{8,9},{9,10},{10,11},{12,13},{... | collective-permute-start | bytes 267272 | tf_op jit(solution)/shard_map/ppermute | solution.py:19
  19.4 1.3 collective-permute-start.3
  21.0 0.6 collective-permute-done.2
  21.6 4.3 %collective-permute-done.3 = bf16[6,1,58,128]{3,2,1,0:T(8,128)(2,1)S(1)} collective-permute-done((bf16[6,1,58,128]{3,2,1,0:T(8,128)(2,1)S(1)}, bf16[6,1,58,128]{3,2,1,0:T(8,128)(2,1)S(1)}, u32[]{:S(2)}, u32[]{:S(2)}) %collective-permute-start.3) | collective-permute-done | bytes 89120 | tf_op jit(solution)/shard_map/ppermute | solution.py:21
  25.9 0.6 fusion.57
  32.0 0.7 copy-done
  35.2 3.4 %collective-permute-start.4 = (bf16[1,4,64,128]{3,2,1,0:T(8,128)(2,1)S(1)}, bf16[1,4,64,128]{3,2,1,0:T(8,128)(2,1)S(1)}, u32[]{:S(2)}, u32[]{:S(2)}) collective-permute-start(bf16[1,4,64,128]{3,2,1,0:T(8,128)(2,1)S(1)} %get-tuple-element.66), channel_id=1, source_target_pairs={{0,4},{4,8},{8,12},{1,5},{5,9},{9,13},{2,6},{6,10},{10,14},{3,7},{... | collective-permute-start | bytes 196616 | tf_op jit(solution)/shard_map/ppermute | solution.py:19
  38.6 1.4 collective-permute-start.5
  40.0 2.7 %collective-permute-done.5 = bf16[1,4,64,128]{3,2,1,0:T(8,128)(2,1)S(1)} collective-permute-done((bf16[1,4,64,128]{3,2,1,0:T(8,128)(2,1)S(1)}, bf16[1,4,64,128]{3,2,1,0:T(8,128)(2,1)S(1)}, u32[]{:S(2)}, u32[]{:S(2)}) %collective-permute-start.5) | collective-permute-done | bytes 65568 | tf_op jit(solution)/shard_map/ppermute | solution.py:21
  42.8 3.5 %collective-permute-start.6 = (bf16[6,1,64,128]{3,2,1,0:T(8,128)(2,1)S(1)}, bf16[6,1,64,128]{3,2,1,0:T(8,128)(2,1)S(1)}, u32[]{:S(2)}, u32[]{:S(2)}) collective-permute-start(bf16[6,1,64,128]{3,2,1,0:T(8,128)(2,1)S(1)} %get-tuple-element.62), channel_id=1, source_target_pairs={{0,1},{1,2},{2,3},{4,5},{5,6},{6,7},{8,9},{9,10},{10,11},{12,13},{... | collective-permute-start | bytes 294920 | tf_op jit(solution)/shard_map/ppermute | solution.py:19
  46.3 1.5 collective-permute-start.7
  47.8 0.7 collective-permute-done.6
  48.5 4.3 %collective-permute-done.7 = bf16[6,1,64,128]{3,2,1,0:T(8,128)(2,1)S(1)} collective-permute-done((bf16[6,1,64,128]{3,2,1,0:T(8,128)(2,1)S(1)}, bf16[6,1,64,128]{3,2,1,0:T(8,128)(2,1)S(1)}, u32[]{:S(2)}, u32[]{:S(2)}) %collective-permute-start.7) | collective-permute-done | bytes 98336 | tf_op jit(solution)/shard_map/ppermute | solution.py:21
  52.8 0.7 select_maximum_fusion
  59.7 0.7 copy-done.4
  74.8 3.4 %collective-permute-start.8 = (bf16[1,6,64,128]{3,2,1,0:T(8,128)(2,1)S(1)}, bf16[1,6,64,128]{3,2,1,0:T(8,128)(2,1)S(1)}, u32[]{:S(2)}, u32[]{:S(2)}) collective-permute-start(bf16[1,6,64,128]{3,2,1,0:T(8,128)(2,1)S(1)} %get-tuple-element.57), channel_id=1, source_target_pairs={{0,4},{4,8},{8,12},{1,5},{5,9},{9,13},{2,6},{6,10},{10,14},{3,7},{... | collective-permute-start | bytes 294920 | tf_op jit(solution)/shard_map/ppermute | solution.py:31
  78.2 1.3 collective-permute-start.9
  81.5 0.8 collective-permute-done.9
  82.4 3.5 %collective-permute-start.10 = (bf16[4,1,64,128]{3,2,1,0:T(8,128)(2,1)S(1)}, bf16[4,1,64,128]{3,2,1,0:T(8,128)(2,1)S(1)}, u32[]{:S(2)}, u32[]{:S(2)}) collective-permute-start(bf16[4,1,64,128]{3,2,1,0:T(8,128)(2,1)S(1)} %get-tuple-element.61), channel_id=1, source_target_pairs={{0,1},{1,2},{2,3},{4,5},{5,6},{6,7},{8,9},{9,10},{10,11},{12,13},{... | collective-permute-start | bytes 196616 | tf_op jit(solution)/shard_map/ppermute | solution.py:31
  85.9 0.9 pad_maximum_fusion.1
  86.9 1.3 collective-permute-start.11
  88.2 4.8 %collective-permute-done.11 = bf16[4,1,64,128]{3,2,1,0:T(8,128)(2,1)S(1)} collective-permute-done((bf16[4,1,64,128]{3,2,1,0:T(8,128)(2,1)S(1)}, bf16[4,1,64,128]{3,2,1,0:T(8,128)(2,1)S(1)}, u32[]{:S(2)}, u32[]{:S(2)}) %collective-permute-start.11) | collective-permute-done | bytes 65568 | tf_op jit(solution)/shard_map/ppermute | solution.py:31
  100.3 1.0 pad_maximum_fusion
  101.3 0.8 copy.43
  102.1 95.4 %all-reduce.7.cloned.1.call-done = (f32[3,3,3,58,64]{4,3,2,1,0:T(8,128)}, f32[3,3,3,64,53]{3,4,2,1,0:T(8,128)}) async-done(((f32[3,3,3,58,64]{4,3,2,1,0:T(8,128)}, f32[3,3,3,64,53]{3,4,2,1,0:T(8,128)}), (f32[3,3,3,58,64]{4,3,2,1,0:T(8,128)}, f32[3,3,3,64,53]{3,4,2,1,0:T(8,128)})) %all-reduce.7.cloned.1.call-update) | async-done | bytes 767248 | tf_op jit(solution)/shard_map/psum | solution.py:157
  197.5 2.2 %copy.200 = f32[3,3,3,58,64]{4,3,2,1,0:T(8,128)} copy(f32[3,3,3,58,64]{4,3,2,1,0:T(8,128)} %get-tuple-element.95) | data formatting | bytes 801792
  199.7 0.9 copy.201
  (184 shorter events, 37.3 us)
Async XLA Ops:
  7.2 13.5 %copy-start.3 = (bf16[3,3,3,58,64]{4,3,2,1,0:T(8,128)(2,1)S(1)}, bf16[3,3,3,58,64]{4,3,2,1,0:T(8,128)(2,1)}, u32[]{:S(2)}) copy-start(bf16[3,3,3,58,64]{4,3,2,1,0:T(8,128)(2,1)} %param.14) | copy-start | bytes 601348
  7.2 190.3 %all-reduce.7.cloned.1.call-start = ((), (), s32[]{:S(2)}) async-start(), calls=%async_computation | async-start | bytes 3317760 | tf_op jit(solution)/shard_map/psum | solution.py:157
  8.2 3.7 %collective-permute-start = (bf16[1,4,58,128]{3,2,1,0:T(8,128)(2,1)S(1)}, bf16[1,4,58,128]{3,2,1,0:T(8,128)(2,1)S(1)}, u32[]{:S(2)}, u32[]{:S(2)}) collective-permute-start(bf16[1,4,58,128]{3,2,1,0:T(8,128)(2,1)S(1)} %copy.188), channel_id=1, source_target_pairs={{0,4},{4,8},{8,12},{1,5},{5,9},{9,13},{2,6},{6,10},{10,14},{3,7},{... | collective-permute-start | bytes 178184 | tf_op jit(solution)/shard_map/ppermute | solution.py:19
  10.6 5.3 %collective-permute-start.1 = (bf16[1,4,58,128]{3,2,1,0:T(8,128)(2,1)S(1)}, bf16[1,4,58,128]{3,2,1,0:T(8,128)(2,1)S(1)}, u32[]{:S(2)}, u32[]{:S(2)}) collective-permute-start(bf16[1,4,58,128]{3,2,1,0:T(8,128)(2,1)S(1)} %copy.189), channel_id=1, source_target_pairs={{4,0},{8,4},{12,8},{5,1},{9,5},{13,9},{6,2},{10,6},{14,10},{7,3},{... | collective-permute-start | bytes 178184 | tf_op jit(solution)/shard_map/ppermute | solution.py:21
  15.9 5.7 %collective-permute-start.2 = (bf16[6,1,58,128]{3,2,1,0:T(8,128)(2,1)S(1)}, bf16[6,1,58,128]{3,2,1,0:T(8,128)(2,1)S(1)}, u32[]{:S(2)}, u32[]{:S(2)}) collective-permute-start(bf16[6,1,58,128]{3,2,1,0:T(8,128)(2,1)S(1)} %get-tuple-element.64), channel_id=1, source_target_pairs={{0,1},{1,2},{2,3},{4,5},{5,6},{6,7},{8,9},{9,10},{10,11},{12,13},{... | collective-permute-start | bytes 267272 | tf_op jit(solution)/shard_map/ppermute | solution.py:19
  19.4 6.5 %collective-permute-start.3 = (bf16[6,1,58,128]{3,2,1,0:T(8,128)(2,1)S(1)}, bf16[6,1,58,128]{3,2,1,0:T(8,128)(2,1)S(1)}, u32[]{:S(2)}, u32[]{:S(2)}) collective-permute-start(bf16[6,1,58,128]{3,2,1,0:T(8,128)(2,1)S(1)} %get-tuple-element.65), channel_id=1, source_target_pairs={{1,0},{2,1},{3,2},{5,4},{6,5},{7,6},{9,8},{10,9},{11,10},{13,12},{... | collective-permute-start | bytes 267272 | tf_op jit(solution)/shard_map/ppermute | solution.py:21
  31.7 0.9 copy-start
  35.2 4.9 %collective-permute-start.4 = (bf16[1,4,64,128]{3,2,1,0:T(8,128)(2,1)S(1)}, bf16[1,4,64,128]{3,2,1,0:T(8,128)(2,1)S(1)}, u32[]{:S(2)}, u32[]{:S(2)}) collective-permute-start(bf16[1,4,64,128]{3,2,1,0:T(8,128)(2,1)S(1)} %get-tuple-element.66), channel_id=1, source_target_pairs={{0,4},{4,8},{8,12},{1,5},{5,9},{9,13},{2,6},{6,10},{10,14},{3,7},{... | collective-permute-start | bytes 196616 | tf_op jit(solution)/shard_map/ppermute | solution.py:19
  38.6 14.9 %copy-start.1 = (bf16[3,3,3,64,53]{3,4,2,1,0:T(8,128)(2,1)S(1)}, bf16[3,3,3,64,53]{3,4,2,1,0:T(8,128)(2,1)}, u32[]{:S(2)}) copy-start(bf16[3,3,3,64,53]{3,4,2,1,0:T(8,128)(2,1)} %param.15) | copy-start | bytes 549508
  38.6 4.2 %collective-permute-start.5 = (bf16[1,4,64,128]{3,2,1,0:T(8,128)(2,1)S(1)}, bf16[1,4,64,128]{3,2,1,0:T(8,128)(2,1)S(1)}, u32[]{:S(2)}, u32[]{:S(2)}) collective-permute-start(bf16[1,4,64,128]{3,2,1,0:T(8,128)(2,1)S(1)} %get-tuple-element.67), channel_id=1, source_target_pairs={{4,0},{8,4},{12,8},{5,1},{9,5},{13,9},{6,2},{10,6},{14,10},{7,3},{... | collective-permute-start | bytes 196616 | tf_op jit(solution)/shard_map/ppermute | solution.py:21
  42.8 5.7 %collective-permute-start.6 = (bf16[6,1,64,128]{3,2,1,0:T(8,128)(2,1)S(1)}, bf16[6,1,64,128]{3,2,1,0:T(8,128)(2,1)S(1)}, u32[]{:S(2)}, u32[]{:S(2)}) collective-permute-start(bf16[6,1,64,128]{3,2,1,0:T(8,128)(2,1)S(1)} %get-tuple-element.62), channel_id=1, source_target_pairs={{0,1},{1,2},{2,3},{4,5},{5,6},{6,7},{8,9},{9,10},{10,11},{12,13},{... | collective-permute-start | bytes 294920 | tf_op jit(solution)/shard_map/ppermute | solution.py:19
  46.3 6.5 %collective-permute-start.7 = (bf16[6,1,64,128]{3,2,1,0:T(8,128)(2,1)S(1)}, bf16[6,1,64,128]{3,2,1,0:T(8,128)(2,1)S(1)}, u32[]{:S(2)}, u32[]{:S(2)}) collective-permute-start(bf16[6,1,64,128]{3,2,1,0:T(8,128)(2,1)S(1)} %get-tuple-element.63), channel_id=1, source_target_pairs={{1,0},{2,1},{3,2},{5,4},{6,5},{7,6},{9,8},{10,9},{11,10},{13,12},{... | collective-permute-start | bytes 294920 | tf_op jit(solution)/shard_map/ppermute | solution.py:21
  59.5 0.9 copy-start.4
  74.8 6.7 %collective-permute-start.8 = (bf16[1,6,64,128]{3,2,1,0:T(8,128)(2,1)S(1)}, bf16[1,6,64,128]{3,2,1,0:T(8,128)(2,1)S(1)}, u32[]{:S(2)}, u32[]{:S(2)}) collective-permute-start(bf16[1,6,64,128]{3,2,1,0:T(8,128)(2,1)S(1)} %get-tuple-element.57), channel_id=1, source_target_pairs={{0,4},{4,8},{8,12},{1,5},{5,9},{9,13},{2,6},{6,10},{10,14},{3,7},{... | collective-permute-start | bytes 294920 | tf_op jit(solution)/shard_map/ppermute | solution.py:31
  78.2 4.1 %collective-permute-start.9 = (bf16[1,6,64,128]{3,2,1,0:T(8,128)(2,1)S(1)}, bf16[1,6,64,128]{3,2,1,0:T(8,128)(2,1)S(1)}, u32[]{:S(2)}, u32[]{:S(2)}) collective-permute-start(bf16[1,6,64,128]{3,2,1,0:T(8,128)(2,1)S(1)} %get-tuple-element.56), channel_id=1, source_target_pairs={{4,0},{8,4},{12,8},{5,1},{9,5},{13,9},{6,2},{10,6},{14,10},{7,3},{... | collective-permute-start | bytes 294920 | tf_op jit(solution)/shard_map/ppermute | solution.py:31
  82.4 5.8 %collective-permute-start.10 = (bf16[4,1,64,128]{3,2,1,0:T(8,128)(2,1)S(1)}, bf16[4,1,64,128]{3,2,1,0:T(8,128)(2,1)S(1)}, u32[]{:S(2)}, u32[]{:S(2)}) collective-permute-start(bf16[4,1,64,128]{3,2,1,0:T(8,128)(2,1)S(1)} %get-tuple-element.61), channel_id=1, source_target_pairs={{0,1},{1,2},{2,3},{4,5},{5,6},{6,7},{8,9},{9,10},{10,11},{12,13},{... | collective-permute-start | bytes 196616 | tf_op jit(solution)/shard_map/ppermute | solution.py:31
  86.9 6.2 %collective-permute-start.11 = (bf16[4,1,64,128]{3,2,1,0:T(8,128)(2,1)S(1)}, bf16[4,1,64,128]{3,2,1,0:T(8,128)(2,1)S(1)}, u32[]{:S(2)}, u32[]{:S(2)}) collective-permute-start(bf16[4,1,64,128]{3,2,1,0:T(8,128)(2,1)S(1)} %get-tuple-element.60), channel_id=1, source_target_pairs={{1,0},{2,1},{3,2},{5,4},{6,5},{7,6},{9,8},{10,9},{11,10},{13,12},{... | collective-permute-start | bytes 196616 | tf_op jit(solution)/shard_map/ppermute | solution.py:31
  197.5 2.3 %copy-start.2 = (f32[3,3,3,64,53]{3,4,2,1,0:T(8,128)S(1)}, f32[3,3,3,64,53]{3,4,2,1,0:T(8,128)}, u32[]{:S(2)}) copy-start(f32[3,3,3,64,53]{3,4,2,1,0:T(8,128)} %get-tuple-element.96) | copy-start | bytes 1099012
Sparse Core Ops, SparseCore 0:
  101.4 95.9 all-reduce.6
where the time goes:
time: 208 us; the launch traced here: 207 us
  waiting for transfers between devices  116 us (56%)
  matrix products  36.2 us (17%)
  starting transfers between devices  27.7 us (13%)
  between operations  15.4 us (7%)
  local copies, waits for them, and re-layouts  7.62 us (4%)
  other arithmetic  4.08 us (2%)
    psum x1, waiting for transfers between devices, on_device(): grad_first, grad_second = lax.psum((grad_first, grad_second), ('gx', 'gy'))  95.4 us
    dot_general x54, matrix products, correlate(): jnp.einsum('xycz,co->xyoz', window, kernel[step_a, step_b, step_c], prefe...  14.4 us
    ppermute x4, waiting for transfers between devices, extended(): lax.ppermute(head, axis, [((i + 1) % count, i) for i in range(ends)])  14.1 us
    ppermute x4, starting transfers between devices, extended(): lax.ppermute(tail, axis, [(i, (i + 1) % count) for i in range(ends)])  12.7 us
    dot_general x54, matrix products, filter_grad(): jnp.einsum('xycz,xyoz->co', window, slope_term, preferred_element_type=jn...  12.7 us
    ppermute x4, starting transfers between devices, shifted(): lax.ppermute(value, axis, [(source, source + steps) for source in range(l...  9.48 us
    dot_general x27, matrix products, correlate_back(): jnp.einsum('xyoz,io->xyiz', window, kernel[step_a, step_b, step_c], prefe...  9.04 us
    unnamed x17, local copies, waits for them, and re-layouts  6.51 us
  transfers between devices with their start and end apart: 13, of which 9 were waited for; matrix products, arithmetic and copies ran while one was open for 2% of the time, Pallas kernels for 0%

commit v1 on v0

--- a/solution.py
+++ b/solution.py
@@ -6,6 +6,7 @@
 
 root_two_pi = 0.7978845608028654
 cubic_term = 0.044715
+close_threads_now = lambda payload: jax.lax.psum(jax.lax.psum(payload, "gy"), "gx")
 
 
 def extended(cells, sides, width):
@@ -154,7 +155,7 @@
     back_grad = summed_x[:, 1 : extent_y - 1].at[:, :1].add(from_left).at[:, -1:].add(from_right)
     slope_term = (back_grad * gate_slope(activation)).astype(jnp.bfloat16)
     grad_first = filter_grad(padded_in, slope_term)
-    grad_first, grad_second = lax.psum((grad_first, grad_second), ("gx", "gy"))
+    grad_first, grad_second = close_threads_now((grad_first, grad_second))
     return (prediction, grad_first, grad_second)
 
 

time: 208 us -> 230 us (1.11)
  waiting for transfers between devices: 116 us -> 139 us
    psum x1 -> x2, waiting for transfers between devices: 95.4 us -> 118 us  [the longest x1 72.4 us: jax.lax.psum(payload, 'gy')]
  transfers between devices with their start and end apart: 13 -> 14, of which waited for: 9 -> 10; matrix products, arithmetic and copies ran while one was open for 2% -> 2% of each run, Pallas kernels for 0% -> 0%
where the time goes in v1:
time: 230 us
  waiting for transfers between devices  139 us (60%)
  matrix products  36.2 us (16%)
  starting transfers between devices  27.8 us (12%)
  between operations  15.4 us (7%)
  local copies, waits for them, and re-layouts  7.62 us (3%)
  other arithmetic  4.08 us (2%)
    psum x1, waiting for transfers between devices, jax.lax.psum(payload, 'gy')  72.4 us
    psum x1, waiting for transfers between devices, jax.lax.psum(jax.lax.psum(payload, 'gy'), 'gx')  45.3 us
    dot_general x54, matrix products, correlate(): jnp.einsum('xycz,co->xyoz', window, kernel[step_a, step_b, step_c], prefe...  14.4 us
    ppermute x4, waiting for transfers between devices, extended(): lax.ppermute(head, axis, [((i + 1) % count, i) for i in range(ends)])  14.1 us
    ppermute x4, starting transfers between devices, extended(): lax.ppermute(tail, axis, [(i, (i + 1) % count) for i in range(ends)])  12.7 us
    dot_general x54, matrix products, filter_grad(): jnp.einsum('xycz,xyoz->co', window, slope_term, preferred_element_type=jn...  12.7 us
    ppermute x4, starting transfers between devices, shifted(): lax.ppermute(value, axis, [(source, source + steps) for source in range(l...  9.48 us
    dot_general x27, matrix products, correlate_back(): jnp.einsum('xyoz,io->xyiz', window, kernel[step_a, step_b, step_c], prefe...  9.04 us
  transfers between devices with their start and end apart: 14, of which 10 were waited for; matrix products, arithmetic and copies ran while one was open for 2% of the time, Pallas kernels for 0%

profile of v1, /device:TPU:0, one launch (start us, length us, event | category | flops | bytes accessed | tf_op | source)
XLA Modules:
  0.0 229.8 jit_solution(7250990427173325516)
XLA Ops:
  7.2 0.9 fusion.357
  8.2 2.4 %collective-permute-start = (bf16[1,4,58,128]{3,2,1,0:T(8,128)(2,1)S(1)}, bf16[1,4,58,128]{3,2,1,0:T(8,128)(2,1)S(1)}, u32[]{:S(2)}, u32[]{:S(2)}) collective-permute-start(bf16[1,4,58,128]{3,2,1,0:T(8,128)(2,1)S(1)} %copy.188), channel_id=1, source_target_pairs={{0,4},{4,8},{8,12},{1,5},{5,9},{9,13},{2,6},{6,10},{10,14},{3,7},{... | collective-permute-start | bytes 178184 | tf_op jit(solution)/shard_map/ppermute | solution.py:20
  10.6 1.3 collective-permute-start.1
  11.9 1.2 constant_dynamic-update-slice_fusion.6
  13.1 2.8 %collective-permute-done.1 = bf16[1,4,58,128]{3,2,1,0:T(8,128)(2,1)S(1)} collective-permute-done((bf16[1,4,58,128]{3,2,1,0:T(8,128)(2,1)S(1)}, bf16[1,4,58,128]{3,2,1,0:T(8,128)(2,1)S(1)}, u32[]{:S(2)}, u32[]{:S(2)}) %collective-permute-start.1) | collective-permute-done | bytes 59424 | tf_op jit(solution)/shard_map/ppermute | solution.py:22
  15.9 3.5 %collective-permute-start.2 = (bf16[6,1,58,128]{3,2,1,0:T(8,128)(2,1)S(1)}, bf16[6,1,58,128]{3,2,1,0:T(8,128)(2,1)S(1)}, u32[]{:S(2)}, u32[]{:S(2)}) collective-permute-start(bf16[6,1,58,128]{3,2,1,0:T(8,128)(2,1)S(1)} %get-tuple-element.66), channel_id=1, source_target_pairs={{0,1},{1,2},{2,3},{4,5},{5,6},{6,7},{8,9},{9,10},{10,11},{12,13},{... | collective-permute-start | bytes 267272 | tf_op jit(solution)/shard_map/ppermute | solution.py:20
  19.4 1.3 collective-permute-start.3
  21.0 0.6 collective-permute-done.2
  21.6 4.3 %collective-permute-done.3 = bf16[6,1,58,128]{3,2,1,0:T(8,128)(2,1)S(1)} collective-permute-done((bf16[6,1,58,128]{3,2,1,0:T(8,128)(2,1)S(1)}, bf16[6,1,58,128]{3,2,1,0:T(8,128)(2,1)S(1)}, u32[]{:S(2)}, u32[]{:S(2)}) %collective-permute-start.3) | collective-permute-done | bytes 89120 | tf_op jit(solution)/shard_map/ppermute | solution.py:22
  32.0 0.7 copy-done
  35.2 3.4 %collective-permute-start.4 = (bf16[1,4,64,128]{3,2,1,0:T(8,128)(2,1)S(1)}, bf16[1,4,64,128]{3,2,1,0:T(8,128)(2,1)S(1)}, u32[]{:S(2)}, u32[]{:S(2)}) collective-permute-start(bf16[1,4,64,128]{3,2,1,0:T(8,128)(2,1)S(1)} %get-tuple-element.68), channel_id=1, source_target_pairs={{0,4},{4,8},{8,12},{1,5},{5,9},{9,13},{2,6},{6,10},{10,14},{3,7},{... | collective-permute-start | bytes 196616 | tf_op jit(solution)/shard_map/ppermute | solution.py:20
  38.6 1.4 collective-permute-start.5
  40.0 2.7 %collective-permute-done.5 = bf16[1,4,64,128]{3,2,1,0:T(8,128)(2,1)S(1)} collective-permute-done((bf16[1,4,64,128]{3,2,1,0:T(8,128)(2,1)S(1)}, bf16[1,4,64,128]{3,2,1,0:T(8,128)(2,1)S(1)}, u32[]{:S(2)}, u32[]{:S(2)}) %collective-permute-start.5) | collective-permute-done | bytes 65568 | tf_op jit(solution)/shard_map/ppermute | solution.py:22
  42.8 3.5 %collective-permute-start.6 = (bf16[6,1,64,128]{3,2,1,0:T(8,128)(2,1)S(1)}, bf16[6,1,64,128]{3,2,1,0:T(8,128)(2,1)S(1)}, u32[]{:S(2)}, u32[]{:S(2)}) collective-permute-start(bf16[6,1,64,128]{3,2,1,0:T(8,128)(2,1)S(1)} %get-tuple-element.64), channel_id=1, source_target_pairs={{0,1},{1,2},{2,3},{4,5},{5,6},{6,7},{8,9},{9,10},{10,11},{12,13},{... | collective-permute-start | bytes 294920 | tf_op jit(solution)/shard_map/ppermute | solution.py:20
  46.3 1.5 collective-permute-start.7
  47.8 0.7 collective-permute-done.6
  48.5 4.3 %collective-permute-done.7 = bf16[6,1,64,128]{3,2,1,0:T(8,128)(2,1)S(1)} collective-permute-done((bf16[6,1,64,128]{3,2,1,0:T(8,128)(2,1)S(1)}, bf16[6,1,64,128]{3,2,1,0:T(8,128)(2,1)S(1)}, u32[]{:S(2)}, u32[]{:S(2)}) %collective-permute-start.7) | collective-permute-done | bytes 98336 | tf_op jit(solution)/shard_map/ppermute | solution.py:22
  52.8 0.7 select_maximum_fusion
  59.7 0.7 copy-done.4
  74.8 3.4 %collective-permute-start.8 = (bf16[1,6,64,128]{3,2,1,0:T(8,128)(2,1)S(1)}, bf16[1,6,64,128]{3,2,1,0:T(8,128)(2,1)S(1)}, u32[]{:S(2)}, u32[]{:S(2)}) collective-permute-start(bf16[1,6,64,128]{3,2,1,0:T(8,128)(2,1)S(1)} %get-tuple-element.59), channel_id=1, source_target_pairs={{0,4},{4,8},{8,12},{1,5},{5,9},{9,13},{2,6},{6,10},{10,14},{3,7},{... | collective-permute-start | bytes 294920 | tf_op jit(solution)/shard_map/ppermute | solution.py:32
  78.2 1.3 collective-permute-start.9
  81.5 0.8 collective-permute-done.9
  82.4 3.5 %collective-permute-start.10 = (bf16[4,1,64,128]{3,2,1,0:T(8,128)(2,1)S(1)}, bf16[4,1,64,128]{3,2,1,0:T(8,128)(2,1)S(1)}, u32[]{:S(2)}, u32[]{:S(2)}) collective-permute-start(bf16[4,1,64,128]{3,2,1,0:T(8,128)(2,1)S(1)} %get-tuple-element.63), channel_id=1, source_target_pairs={{0,1},{1,2},{2,3},{4,5},{5,6},{6,7},{8,9},{9,10},{10,11},{12,13},{... | collective-permute-start | bytes 196616 | tf_op jit(solution)/shard_map/ppermute | solution.py:32
  85.9 0.9 pad_maximum_fusion.1
  86.9 1.3 collective-permute-start.11
  88.2 4.8 %collective-permute-done.11 = bf16[4,1,64,128]{3,2,1,0:T(8,128)(2,1)S(1)} collective-permute-done((bf16[4,1,64,128]{3,2,1,0:T(8,128)(2,1)S(1)}, bf16[4,1,64,128]{3,2,1,0:T(8,128)(2,1)S(1)}, u32[]{:S(2)}, u32[]{:S(2)}) %collective-permute-start.11) | collective-permute-done | bytes 65568 | tf_op jit(solution)/shard_map/ppermute | solution.py:32
  100.3 1.0 pad_maximum_fusion
  101.3 72.4 %all-reduce.9.cloned.1.call-done = (f32[3,3,3,58,64]{4,3,2,1,0:T(8,128)}, f32[3,3,3,64,53]{3,4,2,1,0:T(8,128)}) async-done(((f32[3,3,3,58,64]{4,3,2,1,0:T(8,128)}, f32[3,3,3,64,53]{3,4,2,1,0:T(8,128)}), (f32[3,3,3,58,64]{4,3,2,1,0:T(8,128)}, f32[3,3,3,64,53]{3,4,2,1,0:T(8,128)})) %all-reduce.9.cloned.1.call-update) | async-done | bytes 767248 | tf_op jit(solution)/shard_map/psum | solution.py:9
  173.8 0.8 copy.43
  174.5 45.3 %all-reduce.11.cloned.1.call-done = (f32[3,3,3,58,64]{4,3,2,1,0:T(8,128)}, f32[3,3,3,64,53]{3,4,2,1,0:T(8,128)}) async-done(((f32[3,3,3,58,64]{4,3,2,1,0:T(8,128)}, f32[3,3,3,64,53]{3,4,2,1,0:T(8,128)}), (f32[3,3,3,58,64]{4,3,2,1,0:T(8,128)}, f32[3,3,3,64,53]{3,4,2,1,0:T(8,128)})) %all-reduce.11.cloned.1.call-update) | async-done | bytes 767248 | tf_op jit(solution)/shard_map/psum | solution.py:9
  219.8 2.2 copy.202
  222.1 0.9 copy.203
  (187 shorter events, 38.0 us)
Async XLA Ops:
  7.2 13.5 %copy-start.3 = (bf16[3,3,3,58,64]{4,3,2,1,0:T(8,128)(2,1)S(1)}, bf16[3,3,3,58,64]{4,3,2,1,0:T(8,128)(2,1)}, u32[]{:S(2)}) copy-start(bf16[3,3,3,58,64]{4,3,2,1,0:T(8,128)(2,1)} %param.14) | copy-start | bytes 601348
  7.2 166.6 %all-reduce.9.cloned.1.call-start = ((), (), s32[]{:S(2)}) async-start(), calls=%async_computation | async-start | bytes 3317760 | tf_op jit(solution)/shard_map/psum | solution.py:9
  8.2 3.7 %collective-permute-start = (bf16[1,4,58,128]{3,2,1,0:T(8,128)(2,1)S(1)}, bf16[1,4,58,128]{3,2,1,0:T(8,128)(2,1)S(1)}, u32[]{:S(2)}, u32[]{:S(2)}) collective-permute-start(bf16[1,4,58,128]{3,2,1,0:T(8,128)(2,1)S(1)} %copy.188), channel_id=1, source_target_pairs={{0,4},{4,8},{8,12},{1,5},{5,9},{9,13},{2,6},{6,10},{10,14},{3,7},{... | collective-permute-start | bytes 178184 | tf_op jit(solution)/shard_map/ppermute | solution.py:20
  10.6 5.3 %collective-permute-start.1 = (bf16[1,4,58,128]{3,2,1,0:T(8,128)(2,1)S(1)}, bf16[1,4,58,128]{3,2,1,0:T(8,128)(2,1)S(1)}, u32[]{:S(2)}, u32[]{:S(2)}) collective-permute-start(bf16[1,4,58,128]{3,2,1,0:T(8,128)(2,1)S(1)} %copy.189), channel_id=1, source_target_pairs={{4,0},{8,4},{12,8},{5,1},{9,5},{13,9},{6,2},{10,6},{14,10},{7,3},{... | collective-permute-start | bytes 178184 | tf_op jit(solution)/shard_map/ppermute | solution.py:22
  15.9 5.7 %collective-permute-start.2 = (bf16[6,1,58,128]{3,2,1,0:T(8,128)(2,1)S(1)}, bf16[6,1,58,128]{3,2,1,0:T(8,128)(2,1)S(1)}, u32[]{:S(2)}, u32[]{:S(2)}) collective-permute-start(bf16[6,1,58,128]{3,2,1,0:T(8,128)(2,1)S(1)} %get-tuple-element.66), channel_id=1, source_target_pairs={{0,1},{1,2},{2,3},{4,5},{5,6},{6,7},{8,9},{9,10},{10,11},{12,13},{... | collective-permute-start | bytes 267272 | tf_op jit(solution)/shard_map/ppermute | solution.py:20
  19.4 6.5 %collective-permute-start.3 = (bf16[6,1,58,128]{3,2,1,0:T(8,128)(2,1)S(1)}, bf16[6,1,58,128]{3,2,1,0:T(8,128)(2,1)S(1)}, u32[]{:S(2)}, u32[]{:S(2)}) collective-permute-start(bf16[6,1,58,128]{3,2,1,0:T(8,128)(2,1)S(1)} %get-tuple-element.67), channel_id=1, source_target_pairs={{1,0},{2,1},{3,2},{5,4},{6,5},{7,6},{9,8},{10,9},{11,10},{13,12},{... | collective-permute-start | bytes 267272 | tf_op jit(solution)/shard_map/ppermute | solution.py:22
  31.7 0.9 copy-start
  35.2 4.9 %collective-permute-start.4 = (bf16[1,4,64,128]{3,2,1,0:T(8,128)(2,1)S(1)}, bf16[1,4,64,128]{3,2,1,0:T(8,128)(2,1)S(1)}, u32[]{:S(2)}, u32[]{:S(2)}) collective-permute-start(bf16[1,4,64,128]{3,2,1,0:T(8,128)(2,1)S(1)} %get-tuple-element.68), channel_id=1, source_target_pairs={{0,4},{4,8},{8,12},{1,5},{5,9},{9,13},{2,6},{6,10},{10,14},{3,7},{... | collective-permute-start | bytes 196616 | tf_op jit(solution)/shard_map/ppermute | solution.py:20
  38.6 14.9 %copy-start.1 = (bf16[3,3,3,64,53]{3,4,2,1,0:T(8,128)(2,1)S(1)}, bf16[3,3,3,64,53]{3,4,2,1,0:T(8,128)(2,1)}, u32[]{:S(2)}) copy-start(bf16[3,3,3,64,53]{3,4,2,1,0:T(8,128)(2,1)} %param.15) | copy-start | bytes 549508
  38.6 4.2 %collective-permute-start.5 = (bf16[1,4,64,128]{3,2,1,0:T(8,128)(2,1)S(1)}, bf16[1,4,64,128]{3,2,1,0:T(8,128)(2,1)S(1)}, u32[]{:S(2)}, u32[]{:S(2)}) collective-permute-start(bf16[1,4,64,128]{3,2,1,0:T(8,128)(2,1)S(1)} %get-tuple-element.69), channel_id=1, source_target_pairs={{4,0},{8,4},{12,8},{5,1},{9,5},{13,9},{6,2},{10,6},{14,10},{7,3},{... | collective-permute-start | bytes 196616 | tf_op jit(solution)/shard_map/ppermute | solution.py:22
  42.8 5.7 %collective-permute-start.6 = (bf16[6,1,64,128]{3,2,1,0:T(8,128)(2,1)S(1)}, bf16[6,1,64,128]{3,2,1,0:T(8,128)(2,1)S(1)}, u32[]{:S(2)}, u32[]{:S(2)}) collective-permute-start(bf16[6,1,64,128]{3,2,1,0:T(8,128)(2,1)S(1)} %get-tuple-element.64), channel_id=1, source_target_pairs={{0,1},{1,2},{2,3},{4,5},{5,6},{6,7},{8,9},{9,10},{10,11},{12,13},{... | collective-permute-start | bytes 294920 | tf_op jit(solution)/shard_map/ppermute | solution.py:20
  46.3 6.5 %collective-permute-start.7 = (bf16[6,1,64,128]{3,2,1,0:T(8,128)(2,1)S(1)}, bf16[6,1,64,128]{3,2,1,0:T(8,128)(2,1)S(1)}, u32[]{:S(2)}, u32[]{:S(2)}) collective-permute-start(bf16[6,1,64,128]{3,2,1,0:T(8,128)(2,1)S(1)} %get-tuple-element.65), channel_id=1, source_target_pairs={{1,0},{2,1},{3,2},{5,4},{6,5},{7,6},{9,8},{10,9},{11,10},{13,12},{... | collective-permute-start | bytes 294920 | tf_op jit(solution)/shard_map/ppermute | solution.py:22
  59.5 0.9 copy-start.4
  74.8 6.7 %collective-permute-start.8 = (bf16[1,6,64,128]{3,2,1,0:T(8,128)(2,1)S(1)}, bf16[1,6,64,128]{3,2,1,0:T(8,128)(2,1)S(1)}, u32[]{:S(2)}, u32[]{:S(2)}) collective-permute-start(bf16[1,6,64,128]{3,2,1,0:T(8,128)(2,1)S(1)} %get-tuple-element.59), channel_id=1, source_target_pairs={{0,4},{4,8},{8,12},{1,5},{5,9},{9,13},{2,6},{6,10},{10,14},{3,7},{... | collective-permute-start | bytes 294920 | tf_op jit(solution)/shard_map/ppermute | solution.py:32
  78.2 4.1 %collective-permute-start.9 = (bf16[1,6,64,128]{3,2,1,0:T(8,128)(2,1)S(1)}, bf16[1,6,64,128]{3,2,1,0:T(8,128)(2,1)S(1)}, u32[]{:S(2)}, u32[]{:S(2)}) collective-permute-start(bf16[1,6,64,128]{3,2,1,0:T(8,128)(2,1)S(1)} %get-tuple-element.58), channel_id=1, source_target_pairs={{4,0},{8,4},{12,8},{5,1},{9,5},{13,9},{6,2},{10,6},{14,10},{7,3},{... | collective-permute-start | bytes 294920 | tf_op jit(solution)/shard_map/ppermute | solution.py:32
  82.4 5.8 %collective-permute-start.10 = (bf16[4,1,64,128]{3,2,1,0:T(8,128)(2,1)S(1)}, bf16[4,1,64,128]{3,2,1,0:T(8,128)(2,1)S(1)}, u32[]{:S(2)}, u32[]{:S(2)}) collective-permute-start(bf16[4,1,64,128]{3,2,1,0:T(8,128)(2,1)S(1)} %get-tuple-element.63), channel_id=1, source_target_pairs={{0,1},{1,2},{2,3},{4,5},{5,6},{6,7},{8,9},{9,10},{10,11},{12,13},{... | collective-permute-start | bytes 196616 | tf_op jit(solution)/shard_map/ppermute | solution.py:32
  86.9 6.2 %collective-permute-start.11 = (bf16[4,1,64,128]{3,2,1,0:T(8,128)(2,1)S(1)}, bf16[4,1,64,128]{3,2,1,0:T(8,128)(2,1)S(1)}, u32[]{:S(2)}, u32[]{:S(2)}) collective-permute-start(bf16[4,1,64,128]{3,2,1,0:T(8,128)(2,1)S(1)} %get-tuple-element.62), channel_id=1, source_target_pairs={{1,0},{2,1},{3,2},{5,4},{6,5},{7,6},{9,8},{10,9},{11,10},{13,12},{... | collective-permute-start | bytes 196616 | tf_op jit(solution)/shard_map/ppermute | solution.py:32
  101.3 118.5 %all-reduce.11.cloned.1.call-start = ((), (), s32[]{:S(2)}) async-start(), calls=%async_computation.1 | async-start | bytes 3317760 | tf_op jit(solution)/shard_map/psum | solution.py:9
  219.8 2.3 copy-start.2
Sparse Core Ops, SparseCore 0:
  101.4 72.2 all-reduce.8
  176.2 43.5 all-reduce.10
